TPU v7x, 128 devices: a whole 4x4x4 slice. The times are simulated.
128 devices in a mesh: pa: 32 (over y_lo, x, z), pb: 4 (over y_hi, core).
Axes of the slice: x: 4, y: 4 (y_hi: 2, y_lo: 2; y = y_hi * 2 + y_lo), z: 4, core: 2. Of those that a mesh axis runs over, the one named last changes fastest.
Arguments:
- particles: bfloat16 [98304, 1024], P(('pa', 'pb')), may hold values from -7 to 7
- scores: bfloat16 [98304, 1024], P(('pa', 'pb')), may hold values from -5 to 5
- spread: float32 [1], replicated, may hold values from 256 to 341
- plan: int32 [2, 32], replicated, may hold values from 0 to 31, as said below
Outputs:
- drive: float32 [98304, 1024], P(('pa', 'pb'))
Inputs may be any that keep to these rules, and one draw needn't show every extreme that they name: `plan`: row r lists, for each pa index a, the partner a XOR m_r, where m_r is a round mask of 1 to 31 and different rows have different masks.
All inputs are finite; a program needn't handle non-finite values.
Results may differ from a plain program's by a relative error of at most 0.00033.
Values may be sent and summed in bfloat16 or wider, within the bound.
No kernel may reach another device: no remote copies, remote signals or barrier semaphores. Data moves between devices by JAX's collectives and lax.ppermute only.
A program may use at most 128 MiB of HBM per device.

v0:
```python
import functools

import jax
import jax.numpy as jnp
from jax import lax
from jax.experimental import pallas as pl
from jax.experimental.pallas import tpu as pltpu
from jax.sharding import PartitionSpec as P

LOG2E = 1.4426950408889634
Y_NEXT = 16
PLANE = 16
PRODUCT = (((1,), (1,)), ((), ()))


def fold(square):
    total = square[:, :128]
    for i in range(128, square.shape[1], 128):
        total = total + square[:, i : i + 128]
    return total


def prepare_rows(own_ref, own_square, rate, step, also=None):
    def rows(t, carry):
        at = pl.ds(pl.multiple_of(t * step, step), step)
        mine = own_ref[at, :].astype(jnp.float32)
        square = jnp.sum(fold(mine * mine), axis=1, keepdims=True) * rate
        own_square[at, :] = jnp.broadcast_to(square, (step, 128))
        if also is not None:
            also(at)
        return carry

    lax.fori_loop(0, own_ref.shape[0] // step, rows, 0)


def near_kernel(count, h_ref, own_in, *refs):
    parts, scores = [b.at[0] for b in refs[:count]], [b.at[1] for b in refs[:count]]
    out_ref, total, own_ref, x_buf, d_buf, own_square, col_square, sems, own_sem = refs[count:]
    rows, knots = own_ref.shape
    own_copy = pltpu.make_async_copy(own_in.at[0], own_ref, own_sem)
    own_copy.start()
    scale, rate = 2.0 / h_ref[0], LOG2E / h_ref[0]
    step, tile = 32, 256

    def copies(b):
        return (
            pltpu.make_async_copy(parts[b], x_buf.at[b], sems.at[b, 0]),
            pltpu.make_async_copy(scores[b], d_buf.at[b], sems.at[b, 1]),
        )

    for b in range(count):
        for copy in copies(b):
            copy.start()

    def clear(at):
        out_ref[at, :] = jnp.zeros((step, knots), jnp.float32)
        total[at, :] = jnp.zeros((step, 128), jnp.float32)

    own_copy.wait()
    prepare_rows(own_ref, own_square, rate, step, clear)
    for b in range(count):
        for copy in copies(b):
            copy.wait()

    def block(b, carry):
        def columns(t, carry):
            squares = []
            for u in range(0, 128, step):
                at = pl.ds(pl.multiple_of(t * 128 + u, step), step)
                x = x_buf[b, at, :].astype(jnp.float32)
                d = d_buf[b, at, :].astype(jnp.float32) - scale * x
                d_buf[b, at, :] = d.astype(jnp.bfloat16)
                squares.append(fold(x * x))
            square = jnp.sum(jnp.transpose(jnp.concatenate(squares, axis=0)), axis=0, keepdims=True)
            at = pl.ds(pl.multiple_of(t * 128, 128), 128)
            col_square[:, at] = jnp.broadcast_to(square * rate, (8, 128))
            return carry

        lax.fori_loop(0, rows // 128, columns, 0)

        def one(t, carry):
            at = pl.ds(pl.multiple_of(t // (rows // tile) * tile, tile), tile)
            to = pl.ds(pl.multiple_of(t % (rows // tile) * tile, tile), tile)
            products = lax.dot_general(
                own_ref[at, :], x_buf[b, to, :], PRODUCT, preferred_element_type=jnp.float32
            )
            mine = jnp.concatenate([own_square[at, :]] * (tile // 128), axis=1)
            kernel = jnp.exp2(products * (2.0 * rate) - (mine + col_square[:1, to]))
            total[at, :] += fold(kernel)
            out_ref[at, :] += jnp.dot(
                kernel.astype(jnp.bfloat16), d_buf[b, to, :], preferred_element_type=jnp.float32
            )
            return carry

        lax.fori_loop(0, (rows // tile) ** 2, one, 0)
        return carry

    lax.fori_loop(0, count, block, 0)


def far_kernel(count, choice, last, h_ref, flag_ref, own_in, *refs):
    names = count if choice is None else count + 1
    parts, scores = [b.at[0] for b in refs[:names]], [b.at[1] for b in refs[:names]]
    sum_in, total_in, out_ref = refs[names : names + 3]
    refs = refs[names + 3 :]
    if not last:
        total_out = refs[0]
        refs = refs[1:]
    own_ref, x_buf, s_buf, own_square, total, sems, sum_sems = refs
    rows, knots = own_ref.shape
    own_copy = pltpu.make_async_copy(own_in.at[0], own_ref, sum_sems.at[2])
    own_copy.start()
    scale, rate = 2.0 / h_ref[0], LOG2E / h_ref[0]

    def part_copy(b, source):
        return pltpu.make_async_copy(source, x_buf.at[b], sems.at[b, 0])

    def score_copy(b, source):
        return pltpu.make_async_copy(source, s_buf.at[b], sems.at[b, 1])

    sums = (
        pltpu.make_async_copy(sum_in, out_ref, sum_sems.at[0]),
        pltpu.make_async_copy(total_in, total, sum_sems.at[1]),
    )
    for b in range(count):
        if b == choice:
            for value, n in enumerate((b, count)):
                for copy in (part_copy(b, parts[n]), score_copy(b, scores[n])):
                    pl.when((flag_ref[0] != 0) == bool(value))(copy.start)
        else:
            part_copy(b, parts[b]).start()
            score_copy(b, scores[b]).start()
        if b == 0:
            for copy in sums:
                copy.start()

    own_copy.wait()
    prepare_rows(own_ref, own_square, rate, 256)
    for copy in sums:
        copy.wait()

    def block(b, carry):
        part_copy(b, parts[0]).wait()
        score_copy(b, scores[0]).wait()
        x = x_buf[b].astype(jnp.float32)
        drift = (s_buf[b].astype(jnp.float32) - scale * x).astype(jnp.bfloat16)
        square = jnp.sum(jnp.transpose(fold(x * x)), axis=0, keepdims=True) * rate
        products = lax.dot_general(
            own_ref[...], x_buf[b], PRODUCT, preferred_element_type=jnp.float32
        )
        mine = jnp.concatenate([own_square[...]] * (rows // 128), axis=1)
        kernel = jnp.exp2(products * (2.0 * rate) - (mine + square))
        total[...] += fold(kernel)
        out_ref[...] += jnp.dot(
            kernel.astype(jnp.bfloat16), drift, preferred_element_type=jnp.float32
        )
        return carry

    lax.fori_loop(0, count, block, 0)

    def finish(t, carry):
        at = pl.ds(pl.multiple_of(t * 256, 256), 256)
        if last:
            mine = own_ref[at, :].astype(jnp.float32)
            out_ref[at, :] += scale * mine * jnp.sum(total[at, :], axis=1, keepdims=True)
        else:
            total_out[at, :] = total[at, :]
        return carry

    lax.fori_loop(0, rows // 256, finish, 0)


SMEM = pl.BlockSpec(memory_space=pltpu.SMEM)
VMEM = pl.BlockSpec(memory_space=pltpu.VMEM)
ANY = pl.BlockSpec(memory_space=pl.ANY)


def common(count, rows, knots, mebibytes):
    return dict(
        cost_estimate=pl.CostEstimate(
            flops=4 * count * rows * rows * knots,
            bytes_accessed=4 * (count + 2) * rows * knots,
            transcendentals=count * rows * rows,
        ),
        compiler_params=pltpu.CompilerParams(vmem_limit_bytes=mebibytes * 1024 * 1024),
    )


def near_terms(spread, own, blocks):
    rows, knots = own.shape[1:]
    count = len(blocks)
    return pl.pallas_call(
        functools.partial(near_kernel, count),
        out_shape=[
            jax.ShapeDtypeStruct((rows, knots), jnp.float32),
            jax.ShapeDtypeStruct((rows, 128), jnp.float32),
        ],
        in_specs=[SMEM] + [ANY] * (1 + count),
        out_specs=[VMEM, VMEM],
        scratch_shapes=[
            pltpu.VMEM((rows, knots), jnp.bfloat16),
            pltpu.VMEM((count, rows, knots), jnp.bfloat16),
            pltpu.VMEM((count, rows, knots), jnp.bfloat16),
            pltpu.VMEM((rows, 128), jnp.float32),
            pltpu.VMEM((8, rows), jnp.float32),
            pltpu.SemaphoreType.DMA((count, 2)),
            pltpu.SemaphoreType.DMA,
        ],
        **common(count, rows, knots, 14),
    )(spread, own, *blocks)


def far_terms(spread, flag, own, blocks, running, last, choice=None, other=None):
    rows, knots = own.shape[1:]
    count = len(blocks)
    operands = blocks + ([] if choice is None else [other])
    out_shape = [jax.ShapeDtypeStruct((rows, knots), jnp.float32)]
    if not last:
        out_shape.append(jax.ShapeDtypeStruct((rows, 128), jnp.float32))
    return pl.pallas_call(
        functools.partial(far_kernel, count, choice, last),
        out_shape=out_shape,
        in_specs=[SMEM, SMEM] + [ANY] * (len(operands) + 3),
        out_specs=[VMEM] * len(out_shape),
        scratch_shapes=[
            pltpu.VMEM((rows, knots), jnp.bfloat16),
            pltpu.VMEM((count, rows, knots), jnp.bfloat16),
            pltpu.VMEM((count, rows, knots), jnp.bfloat16),
            pltpu.VMEM((rows, 128), jnp.float32),
            pltpu.VMEM((rows, 128), jnp.float32),
            pltpu.SemaphoreType.DMA((count, 2)),
            pltpu.SemaphoreType.DMA((3,)),
        ],
        **common(count, rows, knots, 13 + 4 * count),
    )(spread, flag, own, *operands, *running)


def hop(block, move, pb_move=0):
    bits = move * lax.axis_size("pb") + pb_move
    if bits == 0:
        return block
    count = lax.axis_size(("pa", "pb"))
    return lax.ppermute(block, ("pa", "pb"), [(i, i ^ bits) for i in range(count)])


def route_kernel(plan_ref, low_move, high_move, high_y, both_y):
    one, two = plan_ref[0, 0], plan_ref[1, 0]
    swap = (one ^ 15) > (two ^ 15)
    low, high = jnp.where(swap, two, one), jnp.where(swap, one, two)
    low_move[0], high_move[0] = low & 15, high & 15
    high_y[0], both_y[0] = high >> 4, low >> 4


def route(plan):
    smem = pl.BlockSpec(memory_space=pltpu.SMEM)
    return pl.pallas_call(
        route_kernel,
        out_shape=[jax.ShapeDtypeStruct((1,), jnp.int32)] * 4,
        in_specs=[smem],
        out_specs=[smem] * 4,
    )(plan)


def per_device(particles, scores, spread, plan):
    own = jnp.stack([particles, scores])
    near_y = hop(own, Y_NEXT)
    mate = hop(own, 0, 1)
    low_move, high_move, high_y, both_y = route(plan)

    def low_exchange(move, spread, own, mate):
        return hop(own, move), near_terms(spread, own, [own, mate])

    low, running = lax.switch(
        low_move[0] - 1,
        [functools.partial(low_exchange, move) for move in range(1, PLANE)],
        *(spread, own, mate),
    )

    late_y, low = lax.optimization_barrier((near_y, low))
    far = hop(late_y, Y_NEXT, 2)
    low_y = hop(low, Y_NEXT)

    def stay(x, y):
        return jnp.where(high_move[0] >= 0, x, y)

    high = lax.switch(
        high_move[0],
        [stay] + [lambda x, y, move=move: hop(x, move) for move in range(1, PLANE)],
        *(jnp.where(high_y[0] == 1, near_y, own), own),
    )

    far, high = lax.optimization_barrier((far, high))
    far_mate = hop(far, 0, 1)
    running = far_terms(
        spread, both_y, own, [low, high], running, last=False, choice=0, other=low_y
    )
    return far_terms(spread, both_y, own, [far, far_mate], running, last=True)[0]


def solution(mesh):
    in_specs = (P(("pa", "pb"), None), P(("pa", "pb"), None), P(), P())
    out_specs = P(("pa", "pb"), None)
    return jax.shard_map(
        per_device, mesh=mesh, in_specs=in_specs, out_specs=out_specs, check_vma=False
    )
```

profile of v0, /device:TPU:1, one launch (start us, length us, event | category | flops | bytes accessed | tf_op | source)
XLA Modules:
  0.0 188.0 jit_solution(922824805917760408)
XLA Ops:
  0.0 3.8 %pad_maximum_fusion.own_in = bf16[2,768,1024]{2,1,0:T(8,128)(2,1)} fusion(bf16[1,768,1024]{2,1,0:T(8,128)(2,1)} %bitcast.6, bf16[1,768,1024]{2,1,0:T(8,128)(2,1)} %bitcast.8), kind=kLoop, calls=%fused_computation.1 | loop fusion | flops 1572864 | bytes 6291456 | tf_op jit(solution)/shard_map/stack | solution.py:265
  3.8 1.4 collective-permute-start.31
  5.2 1.4 collective-permute-start.30
  6.6 1.2 shard_map.46
  8.5 2.4 %collective-permute-done.31 = bf16[2,768,1024]{2,1,0:T(8,128)(2,1)} collective-permute-done((bf16[2,768,1024]{2,1,0:T(8,128)(2,1)}, bf16[2,768,1024]{2,1,0:T(8,128)(2,1)}, u32[]{:S(2)}, u32[]{:S(2)}) %collective-permute-start.31) | collective-permute-done | bytes 3145760 | tf_op jit(solution)/shard_map/ppermute | solution.py:243
  10.9 72.3 %conditional.2 = (bf16[2,768,1024]{2,1,0:T(8,128)(2,1)}, f32[768,1024]{1,0:T(8,128)}, f32[768,128]{1,0:T(8,128)S(1)}) conditional(s32[]{:T(128)} %bitcast.3, (bf16[2,768,1024]{2,1,0:T(8,128)(2,1)}, f32[1]{0:T(128)}, bf16[2,768,1024]{2,1,0:T(8,128)(2,1)}) %tuple.115, (bf16[2,768,1024]{2,1,0:T(8,128)(2,1)}, ...), branch_computations={%region_0.0_spmd, %region_1.0_spmd, %region_2.0_spmd, %region_3.0_... | conditional | flops 4831838208 | bytes 25165888 | solution.py:273
  10.9 3.8 %collective-permute-start.2 = (bf16[2,768,1024]{2,1,0:T(8,128)(2,1)}, bf16[2,768,1024]{2,1,0:T(8,128)(2,1)}, u32[]{:S(2)}, u32[]{:S(2)}) collective-permute-start(bf16[2,768,1024]{2,1,0:T(8,128)(2,1)} %get-tuple-element.143.own_in.refs_0_), channel_id=1, source_target_pairs={{0,12},{1,13},{2,14},{3,15},{4,8},{5,9},{6,10},{7,11},{8,4},{9,5},... | collective-permute-start | bytes 9437192 | tf_op jit(solution)/shard_map/cond/branch_2_fun/ppermute | solution.py:243
  14.7 24.4 %branch_2_fun.1 = (f32[768,1024]{1,0:T(8,128)}, f32[768,128]{1,0:T(8,128)S(1)}) custom-call(f32[1]{0:T(128)} %get-tuple-element.144.h_ref, bf16[2,768,1024]{2,1,0:T(8,128)(2,1)} %get-tuple-element.143.own_in.refs_0_, bf16[2,768,1024]{2,1,0:T(8,128)(2,1)} %get-tuple-element.143.own_in.refs_0_, bf16[2,768,1024]{2,1,0:T(8,128)(2,1)} %get-tuple-element.145.refs_1_), custom_call_target="tpu_custom_call" | custom-call | flops 4831838208 | bytes 12582912 | tf_op jit(solution)/shard_map/cond/branch_2_fun/pallas_call | solution.py:192
  39.1 44.0 %collective-permute-done.2 = bf16[2,768,1024]{2,1,0:T(8,128)(2,1)} collective-permute-done((bf16[2,768,1024]{2,1,0:T(8,128)(2,1)}, bf16[2,768,1024]{2,1,0:T(8,128)(2,1)}, u32[]{:S(2)}, u32[]{:S(2)}) %collective-permute-start.2) | collective-permute-done | bytes 3145760 | tf_op jit(solution)/shard_map/cond/branch_2_fun/ppermute | solution.py:243
  83.2 0.0 collective-permute-done.30
  83.2 0.0 copy-start
  83.2 1.7 copy-done
  84.8 2.7 %collective-permute-start.32 = (bf16[2,768,1024]{2,1,0:T(8,128)(2,1)}, bf16[2,768,1024]{2,1,0:T(8,128)(2,1)S(1)}, u32[]{:S(2)}, u32[]{:S(2)}) collective-permute-start(bf16[2,768,1024]{2,1,0:T(8,128)(2,1)} %copy-done), channel_id=1, source_target_pairs={{0,66},{1,67},{2,64},{3,65},{4,70},{5,71},{6,68},{7,69},{8,74},{9,... | collective-permute-start | bytes 9437192 | tf_op jit(solution)/shard_map/ppermute | solution.py:243
  87.6 0.0 collective-permute-start.34
  88.9 3.2 %broadcast_select_fusion.1 = bf16[2,768,1024]{2,1,0:T(8,128)(2,1)S(1)} fusion(bf16[2,768,1024]{2,1,0:T(8,128)(2,1)} %copy-done, pred[]{:T(512)} %bitcast.5, bf16[1,768,1024]{2,1,0:T(8,128)(2,1)} %bitcast.7, bf16[1,768,1024]{2,1,0:T(8,128)(2,1)} %bitcast.9), kind=kLoop, calls=%fused_computation.2 | loop fusion | flops 3145728 | bytes 9437185 | tf_op jit(solution)/shard_map/jit(_where)/select_n | solution.py:289
  92.1 70.0 %conditional.3 = (bf16[2,768,1024]{2,1,0:T(8,128)(2,1)}) conditional(s32[]{:T(128)} %bitcast.4, (s32[1]{0:T(128)}, bf16[2,768,1024]{2,1,0:T(8,128)(2,1)S(1)}, bf16[2,768,1024]{2,1,0:T(8,128)(2,1)}) %tuple.117, bf16[2,768,1024]{2,1,0:T(8,128)(2,1)S(1)} %broadcast_select_fusion.1, ...), branch_computations={%region_15.16_spmd, %region_16.17_spmd, %region_17.18_spmd, %regio... | conditional | flops 1572865 | bytes 12582960 | solution.py:286
  92.1 1.1 collective-permute-start.16
  93.2 68.9 %collective-permute-done.16 = bf16[2,768,1024]{2,1,0:T(8,128)(2,1)} collective-permute-done((bf16[2,768,1024]{2,1,0:T(8,128)(2,1)S(1)}, bf16[2,768,1024]{2,1,0:T(8,128)(2,1)}, u32[]{:S(2)}, u32[]{:S(2)}) %collective-permute-start.16) | collective-permute-done | bytes 3145760 | tf_op jit(solution)/shard_map/cond/branch_2_fun/ppermute | solution.py:243
  162.1 0.0 collective-permute-done.32.refs_0_
  162.1 2.2 %collective-permute-start.33 = (bf16[2,768,1024]{2,1,0:T(8,128)(2,1)S(1)}, bf16[2,768,1024]{2,1,0:T(8,128)(2,1)S(1)}, u32[]{:S(2)}, u32[]{:S(2)}) collective-permute-start(bf16[2,768,1024]{2,1,0:T(8,128)(2,1)S(1)} %collective-permute-done.32.refs_0_), channel_id=1, source_target_pairs={{0,1},{1,0},{2,3},{3,2},{4,5},{5,4},{6,7},{7,6},{8,9},{9,8},{10,11... | collective-permute-start | bytes 9437192 | tf_op jit(solution)/shard_map/ppermute | solution.py:243
  165.0 0.0 collective-permute-done.34.refs_2_
  165.0 11.0 %shard_map.47 = (f32[768,1024]{1,0:T(8,128)S(1)}, f32[768,128]{1,0:T(8,128)S(1)}) custom-call(f32[1]{0:T(128)S(6)} %copy.66.h_ref, s32[1]{0:T(128)} %get-tuple-element.224.flag_ref, bf16[2,768,1024]{2,1,0:T(8,128)(2,1)} %pad_maximum_fusion.own_in, bf16[2,768,1024]{2,1,0:T(8,128)(2,1)} %get-tuple-element.231.refs_0_, ...), custom_call_target="tpu_custom_call" | custom-call | flops 4831838208 | bytes 12582912 | tf_op jit(solution)/shard_map/pallas_call | solution.py:220
  176.0 0.0 collective-permute-done.33.refs_1_
  176.0 11.8 %shard_map.48 = f32[768,1024]{1,0:T(8,128)} custom-call(f32[1]{0:T(128)S(6)} %copy.66.h_ref, s32[1]{0:T(128)} %get-tuple-element.224.flag_ref, bf16[2,768,1024]{2,1,0:T(8,128)(2,1)} %pad_maximum_fusion.own_in, bf16[2,768,1024]{2,1,0:T(8,128)(2,1)S(1)} %collective-permute-done.32.refs_0_, bf16[2,768,1024]{2,1,0:T(8,128)(2,1)S(1)} %collective-permute-done.33.refs_1_, ...), custom_call_target="tpu_custom_call" | custom-call | flops 4831838208 | bytes 12582912 | tf_op jit(solution)/shard_map/pallas_call | solution.py:220
Async XLA Ops:
  3.8 7.1 %collective-permute-start.31 = (bf16[2,768,1024]{2,1,0:T(8,128)(2,1)}, bf16[2,768,1024]{2,1,0:T(8,128)(2,1)}, u32[]{:S(2)}, u32[]{:S(2)}) collective-permute-start(bf16[2,768,1024]{2,1,0:T(8,128)(2,1)} %pad_maximum_fusion.own_in), channel_id=1, source_target_pairs={{0,1},{1,0},{2,3},{3,2},{4,5},{5,4},{6,7},{7,6},{8,9},{9,8},{10,11... | collective-permute-start | bytes 9437192 | tf_op jit(solution)/shard_map/ppermute | solution.py:243
  5.2 78.0 %collective-permute-start.30 = (bf16[2,768,1024]{2,1,0:T(8,128)(2,1)}, bf16[2,768,1024]{2,1,0:T(8,128)(2,1)S(1)}, u32[]{:S(2)}, u32[]{:S(2)}) collective-permute-start(bf16[2,768,1024]{2,1,0:T(8,128)(2,1)} %pad_maximum_fusion.own_in), channel_id=1, source_target_pairs={{0,64},{1,65},{2,66},{3,67},{4,68},{5,69},{6,70},{7,71},{8,72},{9,... | collective-permute-start | bytes 9437192 | tf_op jit(solution)/shard_map/ppermute | solution.py:243
  10.9 72.3 %collective-permute-start.2 = (bf16[2,768,1024]{2,1,0:T(8,128)(2,1)}, bf16[2,768,1024]{2,1,0:T(8,128)(2,1)}, u32[]{:S(2)}, u32[]{:S(2)}) collective-permute-start(bf16[2,768,1024]{2,1,0:T(8,128)(2,1)} %get-tuple-element.143.own_in.refs_0_), channel_id=1, source_target_pairs={{0,12},{1,13},{2,14},{3,15},{4,8},{5,9},{6,10},{7,11},{8,4},{9,5},... | collective-permute-start | bytes 9437192 | tf_op jit(solution)/shard_map/cond/branch_2_fun/ppermute | solution.py:243
  83.2 1.7 copy-start
  84.8 77.3 %collective-permute-start.32 = (bf16[2,768,1024]{2,1,0:T(8,128)(2,1)}, bf16[2,768,1024]{2,1,0:T(8,128)(2,1)S(1)}, u32[]{:S(2)}, u32[]{:S(2)}) collective-permute-start(bf16[2,768,1024]{2,1,0:T(8,128)(2,1)} %copy-done), channel_id=1, source_target_pairs={{0,66},{1,67},{2,64},{3,65},{4,70},{5,71},{6,68},{7,69},{8,74},{9,... | collective-permute-start | bytes 9437192 | tf_op jit(solution)/shard_map/ppermute | solution.py:243
  87.6 77.4 %collective-permute-start.34 = (bf16[2,768,1024]{2,1,0:T(8,128)(2,1)}, bf16[2,768,1024]{2,1,0:T(8,128)(2,1)}, u32[]{:S(2)}, u32[]{:S(2)}) collective-permute-start(bf16[2,768,1024]{2,1,0:T(8,128)(2,1)} %get-tuple-element.231.refs_0_), channel_id=1, source_target_pairs={{0,64},{1,65},{2,66},{3,67},{4,68},{5,69},{6,70},{7,71},{8,72},{9,... | collective-permute-start | bytes 9437192 | tf_op jit(solution)/shard_map/ppermute | solution.py:243
  92.1 70.0 %collective-permute-start.16 = (bf16[2,768,1024]{2,1,0:T(8,128)(2,1)S(1)}, bf16[2,768,1024]{2,1,0:T(8,128)(2,1)}, u32[]{:S(2)}, u32[]{:S(2)}) collective-permute-start(bf16[2,768,1024]{2,1,0:T(8,128)(2,1)S(1)} %param.17), channel_id=1, source_target_pairs={{0,8},{1,9},{2,10},{3,11},{4,12},{5,13},{6,14},{7,15},{8,0},{9,1},... | collective-permute-start | bytes 9437192 | tf_op jit(solution)/shard_map/cond/branch_2_fun/ppermute | solution.py:243
  162.1 13.9 %collective-permute-start.33 = (bf16[2,768,1024]{2,1,0:T(8,128)(2,1)S(1)}, bf16[2,768,1024]{2,1,0:T(8,128)(2,1)S(1)}, u32[]{:S(2)}, u32[]{:S(2)}) collective-permute-start(bf16[2,768,1024]{2,1,0:T(8,128)(2,1)S(1)} %collective-permute-done.32.refs_0_), channel_id=1, source_target_pairs={{0,1},{1,0},{2,3},{3,2},{4,5},{5,4},{6,7},{7,6},{8,9},{9,8},{10,11... | collective-permute-start | bytes 9437192 | tf_op jit(solution)/shard_map/ppermute | solution.py:243
where the time goes:
time: 186 us; the launch traced here: 188 us
  waiting for transfers between devices  115 us (62%)
  Pallas kernels  48.5 us (26%)
  starting transfers between devices  12.7 us (7%)
  other arithmetic  7.05 us (4%)
  between operations  2.81 us (2%)
    ppermute x7, waiting for transfers between devices, hop(): lax.ppermute(block, ('pa', 'pb'), [(i, i ^ bits) for i in range(count)])  115 us
    pallas_call x1, Pallas kernels, near_terms(): pl.pallas_call(functools.partial(near_kernel, count), out_shape=[jax.Shap...  24.4 us
    pallas_call x2, Pallas kernels, far_terms(): pl.pallas_call(functools.partial(far_kernel, count, choice, last), out_sh...  22.8 us
    ppermute x7, starting transfers between devices, hop(): lax.ppermute(block, ('pa', 'pb'), [(i, i ^ bits) for i in range(count)])  12.7 us
    another operation x1, other arithmetic, per_device(): own = jnp.stack([particles, scores])  3.8 us
  transfers between devices with their start and end apart: 7, of which 3 were waited for; matrix products, arithmetic and copies ran while one was open for 2% of the time, Pallas kernels for 20%

commit v1 on v0

--- a/solution.py
+++ b/solution.py
@@ -33,7 +33,7 @@
     lax.fori_loop(0, own_ref.shape[0] // step, rows, 0)
 
 
-def near_kernel(count, h_ref, own_in, *refs):
+def near_kernel(count, h_ref, skip_ref, own_in, *refs):
     parts, scores = [b.at[0] for b in refs[:count]], [b.at[1] for b in refs[:count]]
     out_ref, total, own_ref, x_buf, d_buf, own_square, col_square, sems, own_sem = refs[count:]
     rows, knots = own_ref.shape
@@ -95,14 +95,18 @@
         lax.fori_loop(0, (rows // tile) ** 2, one, 0)
         return carry
 
-    lax.fori_loop(0, count, block, 0)
-
-
-def far_kernel(count, choice, last, h_ref, flag_ref, own_in, *refs):
-    names = count if choice is None else count + 1
-    parts, scores = [b.at[0] for b in refs[:names]], [b.at[1] for b in refs[:names]]
-    sum_in, total_in, out_ref = refs[names : names + 3]
-    refs = refs[names + 3 :]
+    lax.fori_loop(0, count - skip_ref[0], block, 0)
+
+
+def far_kernel(count, optional, last, h_ref, flag_ref, own_in, *refs):
+    parts, scores = [b.at[0] for b in refs[:count]], [b.at[1] for b in refs[:count]]
+    sum_in, total_in, result = refs[count : count + 3]
+    refs = refs[count + 3 :]
+    if last:
+        out_ref, refs = refs[0], refs[1:]
+    else:
+        out_ref = result
+    begin = 1 - flag_ref[0] if optional else 0
     if not last:
         total_out = refs[0]
         refs = refs[1:]
@@ -122,17 +126,11 @@
         pltpu.make_async_copy(sum_in, out_ref, sum_sems.at[0]),
         pltpu.make_async_copy(total_in, total, sum_sems.at[1]),
     )
+    for copy in sums:
+        copy.start()
     for b in range(count):
-        if b == choice:
-            for value, n in enumerate((b, count)):
-                for copy in (part_copy(b, parts[n]), score_copy(b, scores[n])):
-                    pl.when((flag_ref[0] != 0) == bool(value))(copy.start)
-        else:
-            part_copy(b, parts[b]).start()
-            score_copy(b, scores[b]).start()
-        if b == 0:
-            for copy in sums:
-                copy.start()
+        for copy in (part_copy(b, parts[b]), score_copy(b, scores[b])):
+            pl.when(begin <= b)(copy.start)
 
     own_copy.wait()
     prepare_rows(own_ref, own_square, rate, 256)
@@ -156,18 +154,26 @@
         )
         return carry
 
-    lax.fori_loop(0, count, block, 0)
+    lax.fori_loop(begin, count, block, 0)
+
+    def leave(t):
+        at = pl.ds(pl.multiple_of(t * 256, 256), 256)
+        return pltpu.make_async_copy(out_ref.at[at], result.at[at], sum_sems.at[3 + t])
 
     def finish(t, carry):
         at = pl.ds(pl.multiple_of(t * 256, 256), 256)
         if last:
             mine = own_ref[at, :].astype(jnp.float32)
             out_ref[at, :] += scale * mine * jnp.sum(total[at, :], axis=1, keepdims=True)
+            leave(t).start()
         else:
             total_out[at, :] = total[at, :]
         return carry
 
     lax.fori_loop(0, rows // 256, finish, 0)
+    if last:
+        for t in range(rows // 256):
+            leave(t).wait()
 
 
 SMEM = pl.BlockSpec(memory_space=pltpu.SMEM)
@@ -186,7 +192,7 @@
     )
 
 
-def near_terms(spread, own, blocks):
+def near_terms(spread, skip, own, blocks):
     rows, knots = own.shape[1:]
     count = len(blocks)
     return pl.pallas_call(
@@ -195,7 +201,7 @@
             jax.ShapeDtypeStruct((rows, knots), jnp.float32),
             jax.ShapeDtypeStruct((rows, 128), jnp.float32),
         ],
-        in_specs=[SMEM] + [ANY] * (1 + count),
+        in_specs=[SMEM, SMEM] + [ANY] * (1 + count),
         out_specs=[VMEM, VMEM],
         scratch_shapes=[
             pltpu.VMEM((rows, knots), jnp.bfloat16),
@@ -206,33 +212,33 @@
             pltpu.SemaphoreType.DMA((count, 2)),
             pltpu.SemaphoreType.DMA,
         ],
-        **common(count, rows, knots, 14),
-    )(spread, own, *blocks)
-
-
-def far_terms(spread, flag, own, blocks, running, last, choice=None, other=None):
+        **common(count, rows, knots, 18),
+    )(spread, skip, own, *blocks)
+
+
+def far_terms(spread, flag, own, blocks, running, last, optional=False):
     rows, knots = own.shape[1:]
     count = len(blocks)
-    operands = blocks + ([] if choice is None else [other])
     out_shape = [jax.ShapeDtypeStruct((rows, knots), jnp.float32)]
     if not last:
         out_shape.append(jax.ShapeDtypeStruct((rows, 128), jnp.float32))
     return pl.pallas_call(
-        functools.partial(far_kernel, count, choice, last),
+        functools.partial(far_kernel, count, optional, last),
         out_shape=out_shape,
-        in_specs=[SMEM, SMEM] + [ANY] * (len(operands) + 3),
-        out_specs=[VMEM] * len(out_shape),
-        scratch_shapes=[
+        in_specs=[SMEM, SMEM] + [ANY] * (count + 3),
+        out_specs=[ANY] if last else [VMEM] * 2,
+        scratch_shapes=([pltpu.VMEM((rows, knots), jnp.float32)] if last else [])
+        + [
             pltpu.VMEM((rows, knots), jnp.bfloat16),
             pltpu.VMEM((count, rows, knots), jnp.bfloat16),
             pltpu.VMEM((count, rows, knots), jnp.bfloat16),
             pltpu.VMEM((rows, 128), jnp.float32),
             pltpu.VMEM((rows, 128), jnp.float32),
             pltpu.SemaphoreType.DMA((count, 2)),
-            pltpu.SemaphoreType.DMA((3,)),
+            pltpu.SemaphoreType.DMA((3 + rows // 256,)),
         ],
-        **common(count, rows, knots, 13 + 4 * count),
-    )(spread, flag, own, *operands, *running)
+        **common(count, rows, knots, (17 if last else 13) + 4 * count),
+    )(spread, flag, own, *blocks, *running)
 
 
 def hop(block, move, pb_move=0):
@@ -243,58 +249,64 @@
     return lax.ppermute(block, ("pa", "pb"), [(i, i ^ bits) for i in range(count)])
 
 
-def route_kernel(plan_ref, low_move, high_move, high_y, both_y):
-    one, two = plan_ref[0, 0], plan_ref[1, 0]
+def begin_kernel(plan, particles, scores, out, low_move, high_move, high_y, both_y, sems):
+    copies = [
+        pltpu.make_async_copy(source, out.at[n], sems.at[n])
+        for n, source in enumerate((particles, scores))
+    ]
+    for copy in copies:
+        copy.start()
+    one, two = plan[0, 0], plan[1, 0]
     swap = (one ^ 15) > (two ^ 15)
     low, high = jnp.where(swap, two, one), jnp.where(swap, one, two)
     low_move[0], high_move[0] = low & 15, high & 15
     high_y[0], both_y[0] = high >> 4, low >> 4
-
-
-def route(plan):
-    smem = pl.BlockSpec(memory_space=pltpu.SMEM)
+    for copy in copies:
+        copy.wait()
+
+
+def begin(particles, scores, plan):
     return pl.pallas_call(
-        route_kernel,
-        out_shape=[jax.ShapeDtypeStruct((1,), jnp.int32)] * 4,
-        in_specs=[smem],
-        out_specs=[smem] * 4,
-    )(plan)
+        begin_kernel,
+        out_shape=[jax.ShapeDtypeStruct((2, *particles.shape), particles.dtype)]
+        + [jax.ShapeDtypeStruct((1,), jnp.int32)] * 4,
+        in_specs=[SMEM, ANY, ANY],
+        out_specs=[VMEM] + [SMEM] * 4,
+        scratch_shapes=[pltpu.SemaphoreType.DMA((2,))],
+    )(plan, particles, scores)
 
 
 def per_device(particles, scores, spread, plan):
-    own = jnp.stack([particles, scores])
+    own, low_move, high_move, high_y, both_y = begin(particles, scores, plan)
     near_y = hop(own, Y_NEXT)
-    mate = hop(own, 0, 1)
-    low_move, high_move, high_y, both_y = route(plan)
-
-    def low_exchange(move, spread, own, mate):
-        return hop(own, move), near_terms(spread, own, [own, mate])
-
-    low, running = lax.switch(
-        low_move[0] - 1,
-        [functools.partial(low_exchange, move) for move in range(1, PLANE)],
-        *(spread, own, mate),
-    )
-
-    late_y, low = lax.optimization_barrier((near_y, low))
+
+    low = lax.switch(
+        low_move[0] - 1, [functools.partial(hop, move=move) for move in range(1, PLANE)], own
+    )
+
+    late_y, late_own, low = lax.optimization_barrier((near_y, own, low))
     far = hop(late_y, Y_NEXT, 2)
     low_y = hop(low, Y_NEXT)
-
-    def stay(x, y):
-        return jnp.where(high_move[0] >= 0, x, y)
-
-    high = lax.switch(
+    mate = hop(own, 0, 1)
+    start = jnp.where(high_y[0] == 1, near_y, own)
+
+    def high_exchange(move, start, spread, both_y, own, mate, low):
+        near = near_terms(spread, both_y, own, [own, mate, low])
+        moved = hop(start, move) if move else jnp.where(both_y[0] >= 0, start, own)
+        return moved, near
+
+    high, running = lax.switch(
         high_move[0],
-        [stay] + [lambda x, y, move=move: hop(x, move) for move in range(1, PLANE)],
-        *(jnp.where(high_y[0] == 1, near_y, own), own),
+        [functools.partial(high_exchange, move) for move in range(PLANE)],
+        *(start, spread, both_y, own, mate, low),
     )
 
     far, high = lax.optimization_barrier((far, high))
     far_mate = hop(far, 0, 1)
     running = far_terms(
-        spread, both_y, own, [low, high], running, last=False, choice=0, other=low_y
-    )
-    return far_terms(spread, both_y, own, [far, far_mate], running, last=True)[0]
+        spread, both_y, own, [low_y, high, far], running, last=False, optional=True
+    )
+    return far_terms(spread, both_y, own, [far_mate], running, last=True)[0]
 
 
 def solution(mesh):

time: 186 us -> 178 us (0.957)
  waiting for transfers between devices: 115 us -> 103 us
  Pallas kernels: 48.5 us -> 55.1 us
  other arithmetic: 7.05 us -> 2.22 us
  starting transfers between devices: 12.7 us -> 15.3 us
    ppermute x7, waiting for transfers between devices: 115 us -> 103 us  [hop(): lax.ppermute(block, ('pa', 'pb'), [(i, i ^ bits) for i in range(count)])]
    pallas_call x1, Pallas kernels: 24.4 us -> 32.5 us  [near_terms(): pl.pallas_call(functools.partial(near_kernel, count), out_shape=[jax.Shap...]
    another operation x1 -> x0, other arithmetic: 3.8 us -> none  [per_device(): own = jnp.stack([particles, scores])]
    ppermute x7, starting transfers between devices: 12.7 us -> 15.3 us  [hop(): lax.ppermute(block, ('pa', 'pb'), [(i, i ^ bits) for i in range(count)])]
  transfers between devices with their start and end apart: 7 -> 7, of which waited for: 3 -> 2; matrix products, arithmetic and copies ran while one was open for 2% -> 1% of each run, Pallas kernels for 20% -> 24%
where the time goes in v1:
time: 178 us; the launch traced here: 179 us
  waiting for transfers between devices  103 us (58%)
  Pallas kernels  55.1 us (31%)
  starting transfers between devices  15.3 us (9%)
  between operations  2.73 us (2%)
  other arithmetic  2.22 us (1%)
    ppermute x7, waiting for transfers between devices, hop(): lax.ppermute(block, ('pa', 'pb'), [(i, i ^ bits) for i in range(count)])  103 us
    pallas_call x1, Pallas kernels, near_terms(): pl.pallas_call(functools.partial(near_kernel, count), out_shape=[jax.Shap...  32.5 us
    pallas_call x2, Pallas kernels, far_terms(): pl.pallas_call(functools.partial(far_kernel, count, optional, last), out_...  18.3 us
    ppermute x7, starting transfers between devices, hop(): lax.ppermute(block, ('pa', 'pb'), [(i, i ^ bits) for i in range(count)])  15.3 us
    pallas_call x1, Pallas kernels, begin(): pl.pallas_call(begin_kernel, out_shape=[jax.ShapeDtypeStruct((2, *particl...  4.23 us
  transfers between devices with their start and end apart: 7, of which 2 were waited for; matrix products, arithmetic and copies ran while one was open for 1% of the time, Pallas kernels for 24%

profile of v1, /device:TPU:1, one launch (start us, length us, event | category | flops | bytes accessed | tf_op | source)
XLA Modules:
  0.0 179.0 jit_solution(18137773182047907505)
XLA Ops:
  0.0 4.2 %shard_map.46 = (bf16[2,768,1024]{2,1,0:T(8,128)(2,1)}, s32[1]{0:T(128)}, s32[1]{0:T(128)}, s32[1]{0:T(128)}, s32[1]{0:T(128)}) custom-call(s32[2,32]{1,0:T(2,128)} %plan.1, bf16[768,1024]{1,0:T(8,128)(2,1)} %particles.1, bf16[768,1024]{1,0:T(8,128)(2,1)} %scores.1), custom_call_target="tpu_custom_call" | custom-call | tf_op jit(solution)/shard_map/pallas_call | solution.py:269
  4.2 2.2 %collective-permute-start.30 = (bf16[2,768,1024]{2,1,0:T(8,128)(2,1)}, bf16[2,768,1024]{2,1,0:T(8,128)(2,1)}, u32[]{:S(2)}, u32[]{:S(2)}) collective-permute-start(bf16[2,768,1024]{2,1,0:T(8,128)(2,1)} %get-tuple-element.371.own_in), channel_id=1, source_target_pairs={{0,64},{1,65},{2,66},{3,67},{4,68},{5,69},{6,70},{7,71},{8,72},{9,... | collective-permute-start | bytes 9437192 | tf_op jit(solution)/shard_map/ppermute | solution.py:249
  6.4 1.0 collective-permute-start.32
  8.1 73.0 %conditional.2 = (bf16[2,768,1024]{2,1,0:T(8,128)(2,1)}) conditional(s32[]{:T(128)} %bitcast.1, bf16[2,768,1024]{2,1,0:T(8,128)(2,1)} %get-tuple-element.371.own_in, bf16[2,768,1024]{2,1,0:T(8,128)(2,1)} %get-tuple-element.371.own_in, bf16[2,768,1024]{2,1,0:T(8,128)(2,1)} %get-tuple-element.371.own_in, ...), branch_computations={%region_0.0_spmd, %region_1.0_spmd, %region_2.0_spmd, %region_3.0_... | conditional | bytes 12582960 | solution.py:283
  8.1 4.2 %collective-permute-start.8 = (bf16[2,768,1024]{2,1,0:T(8,128)(2,1)}, bf16[2,768,1024]{2,1,0:T(8,128)(2,1)}, u32[]{:S(2)}, u32[]{:S(2)}) collective-permute-start(bf16[2,768,1024]{2,1,0:T(8,128)(2,1)} %param.8), channel_id=1, source_target_pairs={{0,36},{1,37},{2,38},{3,39},{4,32},{5,33},{6,34},{7,35},{8,44},{9,... | collective-permute-start | bytes 9437192 | tf_op jit(solution)/shard_map/cond/branch_8_fun/ppermute | solution.py:249
  12.3 68.7 %collective-permute-done.8 = bf16[2,768,1024]{2,1,0:T(8,128)(2,1)} collective-permute-done((bf16[2,768,1024]{2,1,0:T(8,128)(2,1)}, bf16[2,768,1024]{2,1,0:T(8,128)(2,1)}, u32[]{:S(2)}, u32[]{:S(2)}) %collective-permute-start.8) | collective-permute-done | bytes 3145760 | tf_op jit(solution)/shard_map/cond/branch_8_fun/ppermute | solution.py:249
  81.0 0.0 collective-permute-done.30
  81.0 1.9 %collective-permute-start.31 = (bf16[2,768,1024]{2,1,0:T(8,128)(2,1)}, bf16[2,768,1024]{2,1,0:T(8,128)(2,1)S(1)}, u32[]{:S(2)}, u32[]{:S(2)}) collective-permute-start(bf16[2,768,1024]{2,1,0:T(8,128)(2,1)} %collective-permute-done.30), channel_id=1, source_target_pairs={{0,66},{1,67},{2,64},{3,65},{4,70},{5,71},{6,68},{7,69},{8,74},{9,... | collective-permute-start | bytes 9437192 | tf_op jit(solution)/shard_map/ppermute | solution.py:249
  82.9 0.4 collective-permute-start.34
  84.5 2.2 %broadcast_select_fusion.1 = bf16[2,768,1024]{2,1,0:T(8,128)(2,1)S(1)} fusion(bf16[2,768,1024]{2,1,0:T(8,128)(2,1)} %collective-permute-done.30, bf16[2,768,1024]{2,1,0:T(8,128)(2,1)} %get-tuple-element.371.own_in, pred[]{:T(512)} %bitcast.3), kind=kLoop, calls=%fused_computation.1 | loop fusion | flops 1572864 | bytes 9437185 | tf_op jit(solution)/shard_map/jit(_where)/select_n | solution.py:291
  86.7 0.0 collective-permute-done.32
  86.7 70.9 %conditional.3 = (bf16[2,768,1024]{2,1,0:T(8,128)(2,1)}, f32[768,1024]{1,0:T(8,128)S(1)}, f32[768,128]{1,0:T(8,128)S(1)}) conditional(s32[]{:T(128)} %bitcast.2, (s32[1]{0:T(128)}, bf16[2,768,1024]{2,1,0:T(8,128)(2,1)S(1)}, bf16[2,768,1024]{2,1,0:T(8,128)(2,1)}, f32[1]{0:T(128)}, bf16[2,768,1024]{2,1,0:T(8,128)(2,1)}, ...), branch_computations={%region_15.16_spmd, %region_16.17_spmd, %region_17.18_spmd, %regio... | conditional | flops 7249330176 | bytes 28311616 | solution.py:298
  87.0 3.5 %collective-permute-start.27 = (bf16[2,768,1024]{2,1,0:T(8,128)(2,1)S(1)}, bf16[2,768,1024]{2,1,0:T(8,128)(2,1)}, u32[]{:S(2)}, u32[]{:S(2)}) collective-permute-start(bf16[2,768,1024]{2,1,0:T(8,128)(2,1)S(1)} %get-tuple-element.332), channel_id=1, source_target_pairs={{0,52},{1,53},{2,54},{3,55},{4,48},{5,49},{6,50},{7,51},{8,60},{9,... | collective-permute-start | bytes 9437192 | tf_op jit(solution)/shard_map/cond/branch_13_fun/ppermute | solution.py:249
  90.5 32.5 %branch_13_fun.1 = (f32[768,1024]{1,0:T(8,128)S(1)}, f32[768,128]{1,0:T(8,128)S(1)}) custom-call(f32[1]{0:T(128)} %get-tuple-element.333.h_ref, s32[1]{0:T(128)} %get-tuple-element.334.skip_ref, bf16[2,768,1024]{2,1,0:T(8,128)(2,1)} %get-tuple-element.335.own_in.refs_0_, bf16[2,768,1024]{2,1,0:T(8,128)(2,1)} %get-tuple-element.335.own_in.refs_0_, ...), custom_call_target="tpu_custom_call" | custom-call | flops 7247757312 | bytes 15728640 | tf_op jit(solution)/shard_map/cond/branch_13_fun/pallas_call | solution.py:198
  123.0 34.7 %collective-permute-done.27 = bf16[2,768,1024]{2,1,0:T(8,128)(2,1)} collective-permute-done((bf16[2,768,1024]{2,1,0:T(8,128)(2,1)S(1)}, bf16[2,768,1024]{2,1,0:T(8,128)(2,1)}, u32[]{:S(2)}, u32[]{:S(2)}) %collective-permute-start.27) | collective-permute-done | bytes 3145760 | tf_op jit(solution)/shard_map/cond/branch_13_fun/ppermute | solution.py:249
  157.7 0.0 collective-permute-done.31.refs_2_
  157.7 2.1 %collective-permute-start.33 = (bf16[2,768,1024]{2,1,0:T(8,128)(2,1)S(1)}, bf16[2,768,1024]{2,1,0:T(8,128)(2,1)S(1)}, u32[]{:S(2)}, u32[]{:S(2)}) collective-permute-start(bf16[2,768,1024]{2,1,0:T(8,128)(2,1)S(1)} %collective-permute-done.31.refs_2_), channel_id=1, source_target_pairs={{0,1},{1,0},{2,3},{3,2},{4,5},{5,4},{6,7},{7,6},{8,9},{9,8},{10,11... | collective-permute-start | bytes 9437192 | tf_op jit(solution)/shard_map/ppermute | solution.py:249
  160.4 0.0 collective-permute-done.34.refs_0_
  160.5 10.4 %shard_map.47 = (f32[768,1024]{1,0:T(8,128)S(1)}, f32[768,128]{1,0:T(8,128)S(1)}) custom-call(f32[1]{0:T(128)S(6)} %copy.68.h_ref, s32[1]{0:T(128)} %get-tuple-element.370.flag_ref, bf16[2,768,1024]{2,1,0:T(8,128)(2,1)} %get-tuple-element.371.own_in, bf16[2,768,1024]{2,1,0:T(8,128)(2,1)} %collective-permute-done.34.refs_0_, ...), custom_call_target="tpu_custom_call" | custom-call | flops 7247757312 | bytes 15728640 | tf_op jit(solution)/shard_map/pallas_call | solution.py:225
  170.8 0.0 collective-permute-done.33.refs_0_
  170.9 8.0 %shard_map.48 = f32[768,1024]{1,0:T(8,128)} custom-call(f32[1]{0:T(128)S(6)} %copy.68.h_ref, s32[1]{0:T(128)} %get-tuple-element.370.flag_ref, bf16[2,768,1024]{2,1,0:T(8,128)(2,1)} %get-tuple-element.371.own_in, bf16[2,768,1024]{2,1,0:T(8,128)(2,1)S(1)} %collective-permute-done.33.refs_0_, f32[768,1024]{1,0:T(8,128)S(1)} %get-tuple-element.382.refs_1_, ...), custom_call_target="tpu_custom_call" | custom-call | flops 2415919104 | bytes 9437184 | tf_op jit(solution)/shard_map/pallas_call | solution.py:225
Async XLA Ops:
  4.2 76.8 %collective-permute-start.30 = (bf16[2,768,1024]{2,1,0:T(8,128)(2,1)}, bf16[2,768,1024]{2,1,0:T(8,128)(2,1)}, u32[]{:S(2)}, u32[]{:S(2)}) collective-permute-start(bf16[2,768,1024]{2,1,0:T(8,128)(2,1)} %get-tuple-element.371.own_in), channel_id=1, source_target_pairs={{0,64},{1,65},{2,66},{3,67},{4,68},{5,69},{6,70},{7,71},{8,72},{9,... | collective-permute-start | bytes 9437192 | tf_op jit(solution)/shard_map/ppermute | solution.py:249
  6.4 80.3 %collective-permute-start.32 = (bf16[2,768,1024]{2,1,0:T(8,128)(2,1)}, bf16[2,768,1024]{2,1,0:T(8,128)(2,1)}, u32[]{:S(2)}, u32[]{:S(2)}) collective-permute-start(bf16[2,768,1024]{2,1,0:T(8,128)(2,1)} %get-tuple-element.371.own_in), channel_id=1, source_target_pairs={{0,1},{1,0},{2,3},{3,2},{4,5},{5,4},{6,7},{7,6},{8,9},{9,8},{10,11... | collective-permute-start | bytes 9437192 | tf_op jit(solution)/shard_map/ppermute | solution.py:249
  8.1 72.9 %collective-permute-start.8 = (bf16[2,768,1024]{2,1,0:T(8,128)(2,1)}, bf16[2,768,1024]{2,1,0:T(8,128)(2,1)}, u32[]{:S(2)}, u32[]{:S(2)}) collective-permute-start(bf16[2,768,1024]{2,1,0:T(8,128)(2,1)} %param.8), channel_id=1, source_target_pairs={{0,36},{1,37},{2,38},{3,39},{4,32},{5,33},{6,34},{7,35},{8,44},{9,... | collective-permute-start | bytes 9437192 | tf_op jit(solution)/shard_map/cond/branch_8_fun/ppermute | solution.py:249
  81.0 76.7 %collective-permute-start.31 = (bf16[2,768,1024]{2,1,0:T(8,128)(2,1)}, bf16[2,768,1024]{2,1,0:T(8,128)(2,1)S(1)}, u32[]{:S(2)}, u32[]{:S(2)}) collective-permute-start(bf16[2,768,1024]{2,1,0:T(8,128)(2,1)} %collective-permute-done.30), channel_id=1, source_target_pairs={{0,66},{1,67},{2,64},{3,65},{4,70},{5,71},{6,68},{7,69},{8,74},{9,... | collective-permute-start | bytes 9437192 | tf_op jit(solution)/shard_map/ppermute | solution.py:249
  82.9 77.5 %collective-permute-start.34 = (bf16[2,768,1024]{2,1,0:T(8,128)(2,1)}, bf16[2,768,1024]{2,1,0:T(8,128)(2,1)}, u32[]{:S(2)}, u32[]{:S(2)}) collective-permute-start(bf16[2,768,1024]{2,1,0:T(8,128)(2,1)} %get-tuple-element.432), channel_id=1, source_target_pairs={{0,64},{1,65},{2,66},{3,67},{4,68},{5,69},{6,70},{7,71},{8,72},{9,... | collective-permute-start | bytes 9437192 | tf_op jit(solution)/shard_map/ppermute | solution.py:249
  87.0 70.7 %collective-permute-start.27 = (bf16[2,768,1024]{2,1,0:T(8,128)(2,1)S(1)}, bf16[2,768,1024]{2,1,0:T(8,128)(2,1)}, u32[]{:S(2)}, u32[]{:S(2)}) collective-permute-start(bf16[2,768,1024]{2,1,0:T(8,128)(2,1)S(1)} %get-tuple-element.332), channel_id=1, source_target_pairs={{0,52},{1,53},{2,54},{3,55},{4,48},{5,49},{6,50},{7,51},{8,60},{9,... | collective-permute-start | bytes 9437192 | tf_op jit(solution)/shard_map/cond/branch_13_fun/ppermute | solution.py:249
  157.7 13.2 %collective-permute-start.33 = (bf16[2,768,1024]{2,1,0:T(8,128)(2,1)S(1)}, bf16[2,768,1024]{2,1,0:T(8,128)(2,1)S(1)}, u32[]{:S(2)}, u32[]{:S(2)}) collective-permute-start(bf16[2,768,1024]{2,1,0:T(8,128)(2,1)S(1)} %collective-permute-done.31.refs_2_), channel_id=1, source_target_pairs={{0,1},{1,0},{2,3},{3,2},{4,5},{5,4},{6,7},{7,6},{8,9},{9,8},{10,11... | collective-permute-start | bytes 9437192 | tf_op jit(solution)/shard_map/ppermute | solution.py:249

commit v2 on v1

--- a/solution.py
+++ b/solution.py
@@ -35,7 +35,7 @@
 
 def near_kernel(count, h_ref, skip_ref, own_in, *refs):
     parts, scores = [b.at[0] for b in refs[:count]], [b.at[1] for b in refs[:count]]
-    out_ref, total, own_ref, x_buf, d_buf, own_square, col_square, sems, own_sem = refs[count:]
+    out_ref, total, own_square, own_ref, x_buf, d_buf, col_square, sems, own_sem = refs[count:]
     rows, knots = own_ref.shape
     own_copy = pltpu.make_async_copy(own_in.at[0], own_ref, own_sem)
     own_copy.start()
@@ -100,8 +100,8 @@
 
 def far_kernel(count, optional, last, h_ref, flag_ref, own_in, *refs):
     parts, scores = [b.at[0] for b in refs[:count]], [b.at[1] for b in refs[:count]]
-    sum_in, total_in, result = refs[count : count + 3]
-    refs = refs[count + 3 :]
+    square_in, sum_in, total_in, result = refs[count : count + 4]
+    refs = refs[count + 4 :]
     if last:
         out_ref, refs = refs[0], refs[1:]
     else:
@@ -125,6 +125,7 @@
     sums = (
         pltpu.make_async_copy(sum_in, out_ref, sum_sems.at[0]),
         pltpu.make_async_copy(total_in, total, sum_sems.at[1]),
+        pltpu.make_async_copy(square_in, own_square, sum_sems.at[3]),
     )
     for copy in sums:
         copy.start()
@@ -133,7 +134,6 @@
             pl.when(begin <= b)(copy.start)
 
     own_copy.wait()
-    prepare_rows(own_ref, own_square, rate, 256)
     for copy in sums:
         copy.wait()
 
@@ -158,7 +158,7 @@
 
     def leave(t):
         at = pl.ds(pl.multiple_of(t * 256, 256), 256)
-        return pltpu.make_async_copy(out_ref.at[at], result.at[at], sum_sems.at[3 + t])
+        return pltpu.make_async_copy(out_ref.at[at], result.at[at], sum_sems.at[4 + t])
 
     def finish(t, carry):
         at = pl.ds(pl.multiple_of(t * 256, 256), 256)
@@ -200,14 +200,14 @@
         out_shape=[
             jax.ShapeDtypeStruct((rows, knots), jnp.float32),
             jax.ShapeDtypeStruct((rows, 128), jnp.float32),
+            jax.ShapeDtypeStruct((rows, 128), jnp.float32),
         ],
         in_specs=[SMEM, SMEM] + [ANY] * (1 + count),
-        out_specs=[VMEM, VMEM],
+        out_specs=[VMEM] * 3,
         scratch_shapes=[
             pltpu.VMEM((rows, knots), jnp.bfloat16),
             pltpu.VMEM((count, rows, knots), jnp.bfloat16),
             pltpu.VMEM((count, rows, knots), jnp.bfloat16),
-            pltpu.VMEM((rows, 128), jnp.float32),
             pltpu.VMEM((8, rows), jnp.float32),
             pltpu.SemaphoreType.DMA((count, 2)),
             pltpu.SemaphoreType.DMA,
@@ -216,7 +216,7 @@
     )(spread, skip, own, *blocks)
 
 
-def far_terms(spread, flag, own, blocks, running, last, optional=False):
+def far_terms(spread, flag, own, own_square, blocks, running, last, optional=False):
     rows, knots = own.shape[1:]
     count = len(blocks)
     out_shape = [jax.ShapeDtypeStruct((rows, knots), jnp.float32)]
@@ -225,7 +225,7 @@
     return pl.pallas_call(
         functools.partial(far_kernel, count, optional, last),
         out_shape=out_shape,
-        in_specs=[SMEM, SMEM] + [ANY] * (count + 3),
+        in_specs=[SMEM, SMEM] + [ANY] * (count + 4),
         out_specs=[ANY] if last else [VMEM] * 2,
         scratch_shapes=([pltpu.VMEM((rows, knots), jnp.float32)] if last else [])
         + [
@@ -235,10 +235,10 @@
             pltpu.VMEM((rows, 128), jnp.float32),
             pltpu.VMEM((rows, 128), jnp.float32),
             pltpu.SemaphoreType.DMA((count, 2)),
-            pltpu.SemaphoreType.DMA((3 + rows // 256,)),
+            pltpu.SemaphoreType.DMA((4 + rows // 256,)),
         ],
         **common(count, rows, knots, (17 if last else 13) + 4 * count),
-    )(spread, flag, own, *blocks, *running)
+    )(spread, flag, own, *blocks, own_square, *running)
 
 
 def hop(block, move, pb_move=0):
@@ -295,7 +295,7 @@
         moved = hop(start, move) if move else jnp.where(both_y[0] >= 0, start, own)
         return moved, near
 
-    high, running = lax.switch(
+    high, (*running, own_square) = lax.switch(
         high_move[0],
         [functools.partial(high_exchange, move) for move in range(PLANE)],
         *(start, spread, both_y, own, mate, low),
@@ -304,9 +304,9 @@
     far, high = lax.optimization_barrier((far, high))
     far_mate = hop(far, 0, 1)
     running = far_terms(
-        spread, both_y, own, [low_y, high, far], running, last=False, optional=True
-    )
-    return far_terms(spread, both_y, own, [far_mate], running, last=True)[0]
+        spread, both_y, own, own_square, [low_y, high, far], running, last=False, optional=True
+    )
+    return far_terms(spread, both_y, own, own_square, [far_mate], running, last=True)[0]
 
 
 def solution(mesh):

time: 178 us -> 184 us (1.034)
  waiting for transfers between devices: 103 us -> 114 us
  Pallas kernels: 55.1 us -> 49.9 us
    ppermute x7, waiting for transfers between devices: 103 us -> 114 us  [hop(): lax.ppermute(block, ('pa', 'pb'), [(i, i ^ bits) for i in range(count)])]
    pallas_call x1, Pallas kernels: 32.5 us -> 24.2 us  [near_terms(): pl.pallas_call(functools.partial(near_kernel, count), out_shape=[jax.Shap...]
    pallas_call x2, Pallas kernels: 18.3 us -> 21.5 us  [far_terms(): pl.pallas_call(functools.partial(far_kernel, count, optional, last), out_...]
  transfers between devices with their start and end apart: 7 -> 7, of which waited for: 2 -> 2; matrix products, arithmetic and copies ran while one was open for 1% -> 1% of each run, Pallas kernels for 24% -> 21%
where the time goes in v2:
time: 184 us; the launch traced here: 186 us
  waiting for transfers between devices  114 us (62%)
  Pallas kernels  49.9 us (27%)
  starting transfers between devices  16.8 us (9%)
  between operations  2.73 us (1%)
  other arithmetic  2.22 us (1%)
    ppermute x7, waiting for transfers between devices, hop(): lax.ppermute(block, ('pa', 'pb'), [(i, i ^ bits) for i in range(count)])  114 us
    pallas_call x1, Pallas kernels, near_terms(): pl.pallas_call(functools.partial(near_kernel, count), out_shape=[jax.Shap...  24.2 us
    pallas_call x2, Pallas kernels, far_terms(): pl.pallas_call(functools.partial(far_kernel, count, optional, last), out_...  21.5 us
    ppermute x7, starting transfers between devices, hop(): lax.ppermute(block, ('pa', 'pb'), [(i, i ^ bits) for i in range(count)])  16.8 us
    pallas_call x1, Pallas kernels, begin(): pl.pallas_call(begin_kernel, out_shape=[jax.ShapeDtypeStruct((2, *particl...  4.23 us
  transfers between devices with their start and end apart: 7, of which 2 were waited for; matrix products, arithmetic and copies ran while one was open for 1% of the time, Pallas kernels for 21%

profile of v2, /device:TPU:1, one launch (start us, length us, event | category | flops | bytes accessed | tf_op | source)
XLA Modules:
  0.0 185.5 jit_solution(14091110079204842402)
XLA Ops:
  0.0 4.2 %shard_map.46 = (bf16[2,768,1024]{2,1,0:T(8,128)(2,1)}, s32[1]{0:T(128)}, s32[1]{0:T(128)}, s32[1]{0:T(128)}, s32[1]{0:T(128)}) custom-call(s32[2,32]{1,0:T(2,128)} %plan.1, bf16[768,1024]{1,0:T(8,128)(2,1)} %particles.1, bf16[768,1024]{1,0:T(8,128)(2,1)} %scores.1), custom_call_target="tpu_custom_call" | custom-call | tf_op jit(solution)/shard_map/pallas_call | solution.py:269
  4.2 2.2 %collective-permute-start.30 = (bf16[2,768,1024]{2,1,0:T(8,128)(2,1)}, bf16[2,768,1024]{2,1,0:T(8,128)(2,1)}, u32[]{:S(2)}, u32[]{:S(2)}) collective-permute-start(bf16[2,768,1024]{2,1,0:T(8,128)(2,1)} %get-tuple-element.388.own_in), channel_id=1, source_target_pairs={{0,64},{1,65},{2,66},{3,67},{4,68},{5,69},{6,70},{7,71},{8,72},{9,... | collective-permute-start | bytes 9437192 | tf_op jit(solution)/shard_map/ppermute | solution.py:249
  6.4 1.0 collective-permute-start.32
  8.1 74.9 %conditional.2 = (bf16[2,768,1024]{2,1,0:T(8,128)(2,1)}) conditional(s32[]{:T(128)} %bitcast.1, bf16[2,768,1024]{2,1,0:T(8,128)(2,1)} %get-tuple-element.388.own_in, bf16[2,768,1024]{2,1,0:T(8,128)(2,1)} %get-tuple-element.388.own_in, bf16[2,768,1024]{2,1,0:T(8,128)(2,1)} %get-tuple-element.388.own_in, ...), branch_computations={%region_0.0_spmd, %region_1.0_spmd, %region_2.0_spmd, %region_3.0_... | conditional | bytes 12582960 | solution.py:283
  8.1 6.0 %collective-permute-start.14 = (bf16[2,768,1024]{2,1,0:T(8,128)(2,1)}, bf16[2,768,1024]{2,1,0:T(8,128)(2,1)}, u32[]{:S(2)}, u32[]{:S(2)}) collective-permute-start(bf16[2,768,1024]{2,1,0:T(8,128)(2,1)} %param.14), channel_id=1, source_target_pairs={{0,60},{1,61},{2,62},{3,63},{4,56},{5,57},{6,58},{7,59},{8,52},{9,... | collective-permute-start | bytes 9437192 | tf_op jit(solution)/shard_map/cond/branch_14_fun/ppermute | solution.py:249
  14.1 68.8 %collective-permute-done.14 = bf16[2,768,1024]{2,1,0:T(8,128)(2,1)} collective-permute-done((bf16[2,768,1024]{2,1,0:T(8,128)(2,1)}, bf16[2,768,1024]{2,1,0:T(8,128)(2,1)}, u32[]{:S(2)}, u32[]{:S(2)}) %collective-permute-start.14) | collective-permute-done | bytes 3145760 | tf_op jit(solution)/shard_map/cond/branch_14_fun/ppermute | solution.py:249
  82.9 0.0 collective-permute-done.30
  82.9 1.9 %collective-permute-start.31 = (bf16[2,768,1024]{2,1,0:T(8,128)(2,1)}, bf16[2,768,1024]{2,1,0:T(8,128)(2,1)S(1)}, u32[]{:S(2)}, u32[]{:S(2)}) collective-permute-start(bf16[2,768,1024]{2,1,0:T(8,128)(2,1)} %collective-permute-done.30), channel_id=1, source_target_pairs={{0,66},{1,67},{2,64},{3,65},{4,70},{5,71},{6,68},{7,69},{8,74},{9,... | collective-permute-start | bytes 9437192 | tf_op jit(solution)/shard_map/ppermute | solution.py:249
  84.8 0.4 collective-permute-start.34
  86.4 2.2 %broadcast_select_fusion.1 = bf16[2,768,1024]{2,1,0:T(8,128)(2,1)S(1)} fusion(bf16[2,768,1024]{2,1,0:T(8,128)(2,1)} %collective-permute-done.30, bf16[2,768,1024]{2,1,0:T(8,128)(2,1)} %get-tuple-element.388.own_in, pred[]{:T(512)} %bitcast.3), kind=kLoop, calls=%fused_computation.1 | loop fusion | flops 1572864 | bytes 9437185 | tf_op jit(solution)/shard_map/jit(_where)/select_n | solution.py:291
  88.6 0.0 collective-permute-done.32
  88.7 72.5 %conditional.3 = (bf16[2,768,1024]{2,1,0:T(8,128)(2,1)}, f32[768,1024]{1,0:T(8,128)S(1)}, f32[768,128]{1,0:T(8,128)S(1)}, f32[768,128]{1,0:T(8,128)S(1)}) conditional(s32[]{:T(128)} %bitcast.2, (s32[1]{0:T(128)}, bf16[2,768,1024]{2,1,0:T(8,128)(2,1)S(1)}, bf16[2,768,1024]{2,1,0:T(8,128)(2,1)}, f32[1]{0:T(128)}, ...), branch_computations={%region_15.16_spmd, %region_16.17_spmd, %region_17.18_spmd, %regio... | conditional | flops 7249330176 | bytes 28311624 | solution.py:298
  88.9 3.3 %collective-permute-start.28 = (bf16[2,768,1024]{2,1,0:T(8,128)(2,1)S(1)}, bf16[2,768,1024]{2,1,0:T(8,128)(2,1)}, u32[]{:S(2)}, u32[]{:S(2)}) collective-permute-start(bf16[2,768,1024]{2,1,0:T(8,128)(2,1)S(1)} %get-tuple-element.354), channel_id=1, source_target_pairs={{0,56},{1,57},{2,58},{3,59},{4,60},{5,61},{6,62},{7,63},{8,48},{9,... | collective-permute-start | bytes 9437192 | tf_op jit(solution)/shard_map/cond/branch_14_fun/ppermute | solution.py:249
  92.2 24.2 %branch_14_fun.1 = (f32[768,1024]{1,0:T(8,128)S(1)}, f32[768,128]{1,0:T(8,128)S(1)}, f32[768,128]{1,0:T(8,128)S(1)}) custom-call(f32[1]{0:T(128)} %get-tuple-element.355.h_ref, s32[1]{0:T(128)} %get-tuple-element.356.skip_ref, bf16[2,768,1024]{2,1,0:T(8,128)(2,1)} %get-tuple-element.357.own_in.refs_0_, ...), custom_call_target="tpu_custom_call" | custom-call | flops 7247757312 | bytes 15728640 | tf_op jit(solution)/shard_map/cond/branch_14_fun/pallas_call | solution.py:198
  116.4 44.8 %collective-permute-done.28 = bf16[2,768,1024]{2,1,0:T(8,128)(2,1)} collective-permute-done((bf16[2,768,1024]{2,1,0:T(8,128)(2,1)S(1)}, bf16[2,768,1024]{2,1,0:T(8,128)(2,1)}, u32[]{:S(2)}, u32[]{:S(2)}) %collective-permute-start.28) | collective-permute-done | bytes 3145760 | tf_op jit(solution)/shard_map/cond/branch_14_fun/ppermute | solution.py:249
  161.1 0.0 collective-permute-done.31.refs_2_
  161.1 2.1 %collective-permute-start.33 = (bf16[2,768,1024]{2,1,0:T(8,128)(2,1)S(1)}, bf16[2,768,1024]{2,1,0:T(8,128)(2,1)S(1)}, u32[]{:S(2)}, u32[]{:S(2)}) collective-permute-start(bf16[2,768,1024]{2,1,0:T(8,128)(2,1)S(1)} %collective-permute-done.31.refs_2_), channel_id=1, source_target_pairs={{0,1},{1,0},{2,3},{3,2},{4,5},{5,4},{6,7},{7,6},{8,9},{9,8},{10,11... | collective-permute-start | bytes 9437192 | tf_op jit(solution)/shard_map/ppermute | solution.py:249
  163.9 0.0 collective-permute-done.34.refs_0_
  163.9 14.0 %shard_map.47 = (f32[768,1024]{1,0:T(8,128)S(1)}, f32[768,128]{1,0:T(8,128)S(1)}) custom-call(f32[1]{0:T(128)S(6)} %copy.84.h_ref, s32[1]{0:T(128)} %get-tuple-element.387.flag_ref, bf16[2,768,1024]{2,1,0:T(8,128)(2,1)} %get-tuple-element.388.own_in, bf16[2,768,1024]{2,1,0:T(8,128)(2,1)} %collective-permute-done.34.refs_0_, ...), custom_call_target="tpu_custom_call" | custom-call | flops 7247757312 | bytes 15728640 | tf_op jit(solution)/shard_map/pallas_call | solution.py:225
  177.9 0.0 collective-permute-done.33.refs_0_
  177.9 7.4 %shard_map.48 = f32[768,1024]{1,0:T(8,128)} custom-call(f32[1]{0:T(128)S(6)} %copy.84.h_ref, s32[1]{0:T(128)} %get-tuple-element.387.flag_ref, bf16[2,768,1024]{2,1,0:T(8,128)(2,1)} %get-tuple-element.388.own_in, bf16[2,768,1024]{2,1,0:T(8,128)(2,1)S(1)} %collective-permute-done.33.refs_0_, f32[768,128]{1,0:T(8,128)S(1)} %get-tuple-element.396.refs_3_.refs_1_, ...), custom_call_target="tpu_custom_call" | custom-call | flops 2415919104 | bytes 9437184 | tf_op jit(solution)/shard_map/pallas_call | solution.py:225
Async XLA Ops:
  4.2 78.7 %collective-permute-start.30 = (bf16[2,768,1024]{2,1,0:T(8,128)(2,1)}, bf16[2,768,1024]{2,1,0:T(8,128)(2,1)}, u32[]{:S(2)}, u32[]{:S(2)}) collective-permute-start(bf16[2,768,1024]{2,1,0:T(8,128)(2,1)} %get-tuple-element.388.own_in), channel_id=1, source_target_pairs={{0,64},{1,65},{2,66},{3,67},{4,68},{5,69},{6,70},{7,71},{8,72},{9,... | collective-permute-start | bytes 9437192 | tf_op jit(solution)/shard_map/ppermute | solution.py:249
  6.4 82.2 %collective-permute-start.32 = (bf16[2,768,1024]{2,1,0:T(8,128)(2,1)}, bf16[2,768,1024]{2,1,0:T(8,128)(2,1)}, u32[]{:S(2)}, u32[]{:S(2)}) collective-permute-start(bf16[2,768,1024]{2,1,0:T(8,128)(2,1)} %get-tuple-element.388.own_in), channel_id=1, source_target_pairs={{0,1},{1,0},{2,3},{3,2},{4,5},{5,4},{6,7},{7,6},{8,9},{9,8},{10,11... | collective-permute-start | bytes 9437192 | tf_op jit(solution)/shard_map/ppermute | solution.py:249
  8.1 74.8 %collective-permute-start.14 = (bf16[2,768,1024]{2,1,0:T(8,128)(2,1)}, bf16[2,768,1024]{2,1,0:T(8,128)(2,1)}, u32[]{:S(2)}, u32[]{:S(2)}) collective-permute-start(bf16[2,768,1024]{2,1,0:T(8,128)(2,1)} %param.14), channel_id=1, source_target_pairs={{0,60},{1,61},{2,62},{3,63},{4,56},{5,57},{6,58},{7,59},{8,52},{9,... | collective-permute-start | bytes 9437192 | tf_op jit(solution)/shard_map/cond/branch_14_fun/ppermute | solution.py:249
  82.9 78.2 %collective-permute-start.31 = (bf16[2,768,1024]{2,1,0:T(8,128)(2,1)}, bf16[2,768,1024]{2,1,0:T(8,128)(2,1)S(1)}, u32[]{:S(2)}, u32[]{:S(2)}) collective-permute-start(bf16[2,768,1024]{2,1,0:T(8,128)(2,1)} %collective-permute-done.30), channel_id=1, source_target_pairs={{0,66},{1,67},{2,64},{3,65},{4,70},{5,71},{6,68},{7,69},{8,74},{9,... | collective-permute-start | bytes 9437192 | tf_op jit(solution)/shard_map/ppermute | solution.py:249
  84.8 79.0 %collective-permute-start.34 = (bf16[2,768,1024]{2,1,0:T(8,128)(2,1)}, bf16[2,768,1024]{2,1,0:T(8,128)(2,1)}, u32[]{:S(2)}, u32[]{:S(2)}) collective-permute-start(bf16[2,768,1024]{2,1,0:T(8,128)(2,1)} %get-tuple-element.466), channel_id=1, source_target_pairs={{0,64},{1,65},{2,66},{3,67},{4,68},{5,69},{6,70},{7,71},{8,72},{9,... | collective-permute-start | bytes 9437192 | tf_op jit(solution)/shard_map/ppermute | solution.py:249
  88.9 72.3 %collective-permute-start.28 = (bf16[2,768,1024]{2,1,0:T(8,128)(2,1)S(1)}, bf16[2,768,1024]{2,1,0:T(8,128)(2,1)}, u32[]{:S(2)}, u32[]{:S(2)}) collective-permute-start(bf16[2,768,1024]{2,1,0:T(8,128)(2,1)S(1)} %get-tuple-element.354), channel_id=1, source_target_pairs={{0,56},{1,57},{2,58},{3,59},{4,60},{5,61},{6,62},{7,63},{8,48},{9,... | collective-permute-start | bytes 9437192 | tf_op jit(solution)/shard_map/cond/branch_14_fun/ppermute | solution.py:249
  161.1 16.8 %collective-permute-start.33 = (bf16[2,768,1024]{2,1,0:T(8,128)(2,1)S(1)}, bf16[2,768,1024]{2,1,0:T(8,128)(2,1)S(1)}, u32[]{:S(2)}, u32[]{:S(2)}) collective-permute-start(bf16[2,768,1024]{2,1,0:T(8,128)(2,1)S(1)} %collective-permute-done.31.refs_2_), channel_id=1, source_target_pairs={{0,1},{1,0},{2,3},{3,2},{4,5},{5,4},{6,7},{7,6},{8,9},{9,8},{10,11... | collective-permute-start | bytes 9437192 | tf_op jit(solution)/shard_map/ppermute | solution.py:249

commit v3 on v2

--- a/solution.py
+++ b/solution.py
@@ -122,8 +122,8 @@
     def score_copy(b, source):
         return pltpu.make_async_copy(source, s_buf.at[b], sems.at[b, 1])
 
+    drive_copy = pltpu.make_async_copy(sum_in, out_ref, sum_sems.at[0])
     sums = (
-        pltpu.make_async_copy(sum_in, out_ref, sum_sems.at[0]),
         pltpu.make_async_copy(total_in, total, sum_sems.at[1]),
         pltpu.make_async_copy(square_in, own_square, sum_sems.at[3]),
     )
@@ -132,6 +132,8 @@
     for b in range(count):
         for copy in (part_copy(b, parts[b]), score_copy(b, scores[b])):
             pl.when(begin <= b)(copy.start)
+        if b == min(1, count - 1):
+            drive_copy.start()
 
     own_copy.wait()
     for copy in sums:
@@ -149,6 +151,7 @@
         mine = jnp.concatenate([own_square[...]] * (rows // 128), axis=1)
         kernel = jnp.exp2(products * (2.0 * rate) - (mine + square))
         total[...] += fold(kernel)
+        pl.when(b == begin)(drive_copy.wait)
         out_ref[...] += jnp.dot(
             kernel.astype(jnp.bfloat16), drift, preferred_element_type=jnp.float32
         )

time: 184 us -> 180 us (0.978); the launches traced: 186 us -> 178 us
  waiting for transfers between devices: 114 us -> 104 us
  Pallas kernels: 49.9 us -> 56.3 us
  starting transfers between devices: 16.8 us -> 13.1 us
    ppermute x7, waiting for transfers between devices: 114 us -> 104 us  [hop(): lax.ppermute(block, ('pa', 'pb'), [(i, i ^ bits) for i in range(count)])]
    pallas_call x1, Pallas kernels: 24.2 us -> 32.5 us  [near_terms(): pl.pallas_call(functools.partial(near_kernel, count), out_shape=[jax.Shap...]
    ppermute x7, starting transfers between devices: 16.8 us -> 13.1 us  [hop(): lax.ppermute(block, ('pa', 'pb'), [(i, i ^ bits) for i in range(count)])]
    pallas_call x2, Pallas kernels: 21.5 us -> 19.6 us  [far_terms(): pl.pallas_call(functools.partial(far_kernel, count, optional, last), out_...]
  transfers between devices with their start and end apart: 7 -> 7, of which waited for: 2 -> 2; matrix products, arithmetic and copies ran while one was open for 1% -> 1% of each run, Pallas kernels for 21% -> 25%
where the time goes in v3:
time: 180 us; the launch traced here: 178 us
  waiting for transfers between devices  104 us (58%)
  Pallas kernels  56.3 us (31%)
  starting transfers between devices  13.1 us (7%)
  between operations  2.73 us (2%)
  other arithmetic  2.23 us (1%)
    ppermute x7, waiting for transfers between devices, hop(): lax.ppermute(block, ('pa', 'pb'), [(i, i ^ bits) for i in range(count)])  104 us
    pallas_call x1, Pallas kernels, near_terms(): pl.pallas_call(functools.partial(near_kernel, count), out_shape=[jax.Shap...  32.5 us
    pallas_call x2, Pallas kernels, far_terms(): pl.pallas_call(functools.partial(far_kernel, count, optional, last), out_...  19.6 us
    ppermute x7, starting transfers between devices, hop(): lax.ppermute(block, ('pa', 'pb'), [(i, i ^ bits) for i in range(count)])  13.1 us
    pallas_call x1, Pallas kernels, begin(): pl.pallas_call(begin_kernel, out_shape=[jax.ShapeDtypeStruct((2, *particl...  4.23 us
  transfers between devices with their start and end apart: 7, of which 2 were waited for; matrix products, arithmetic and copies ran while one was open for 1% of the time, Pallas kernels for 25%

profile of v3, /device:TPU:1, one launch (start us, length us, event | category | flops | bytes accessed | tf_op | source)
XLA Modules:
  0.0 177.9 jit_solution(8901094729870984851)
XLA Ops:
  0.0 4.2 %shard_map.46 = (bf16[2,768,1024]{2,1,0:T(8,128)(2,1)}, s32[1]{0:T(128)}, s32[1]{0:T(128)}, s32[1]{0:T(128)}, s32[1]{0:T(128)}) custom-call(s32[2,32]{1,0:T(2,128)} %plan.1, bf16[768,1024]{1,0:T(8,128)(2,1)} %particles.1, bf16[768,1024]{1,0:T(8,128)(2,1)} %scores.1), custom_call_target="tpu_custom_call" | custom-call | tf_op jit(solution)/shard_map/pallas_call | solution.py:272
  4.2 2.2 %collective-permute-start.30 = (bf16[2,768,1024]{2,1,0:T(8,128)(2,1)}, bf16[2,768,1024]{2,1,0:T(8,128)(2,1)}, u32[]{:S(2)}, u32[]{:S(2)}) collective-permute-start(bf16[2,768,1024]{2,1,0:T(8,128)(2,1)} %get-tuple-element.388.own_in), channel_id=1, source_target_pairs={{0,64},{1,65},{2,66},{3,67},{4,68},{5,69},{6,70},{7,71},{8,72},{9,... | collective-permute-start | bytes 9437192 | tf_op jit(solution)/shard_map/ppermute | solution.py:252
  6.4 1.0 collective-permute-start.32
  8.1 73.0 %conditional.2 = (bf16[2,768,1024]{2,1,0:T(8,128)(2,1)}) conditional(s32[]{:T(128)} %bitcast.1, bf16[2,768,1024]{2,1,0:T(8,128)(2,1)} %get-tuple-element.388.own_in, bf16[2,768,1024]{2,1,0:T(8,128)(2,1)} %get-tuple-element.388.own_in, bf16[2,768,1024]{2,1,0:T(8,128)(2,1)} %get-tuple-element.388.own_in, ...), branch_computations={%region_0.0_spmd, %region_1.0_spmd, %region_2.0_spmd, %region_3.0_... | conditional | bytes 12582960 | solution.py:286
  8.1 4.2 %collective-permute-start.8 = (bf16[2,768,1024]{2,1,0:T(8,128)(2,1)}, bf16[2,768,1024]{2,1,0:T(8,128)(2,1)}, u32[]{:S(2)}, u32[]{:S(2)}) collective-permute-start(bf16[2,768,1024]{2,1,0:T(8,128)(2,1)} %param.8), channel_id=1, source_target_pairs={{0,36},{1,37},{2,38},{3,39},{4,32},{5,33},{6,34},{7,35},{8,44},{9,... | collective-permute-start | bytes 9437192 | tf_op jit(solution)/shard_map/cond/branch_8_fun/ppermute | solution.py:252
  12.3 68.7 %collective-permute-done.8 = bf16[2,768,1024]{2,1,0:T(8,128)(2,1)} collective-permute-done((bf16[2,768,1024]{2,1,0:T(8,128)(2,1)}, bf16[2,768,1024]{2,1,0:T(8,128)(2,1)}, u32[]{:S(2)}, u32[]{:S(2)}) %collective-permute-start.8) | collective-permute-done | bytes 3145760 | tf_op jit(solution)/shard_map/cond/branch_8_fun/ppermute | solution.py:252
  81.0 0.0 collective-permute-done.30
  81.0 1.9 %collective-permute-start.31 = (bf16[2,768,1024]{2,1,0:T(8,128)(2,1)}, bf16[2,768,1024]{2,1,0:T(8,128)(2,1)S(1)}, u32[]{:S(2)}, u32[]{:S(2)}) collective-permute-start(bf16[2,768,1024]{2,1,0:T(8,128)(2,1)} %collective-permute-done.30), channel_id=1, source_target_pairs={{0,66},{1,67},{2,64},{3,65},{4,70},{5,71},{6,68},{7,69},{8,74},{9,... | collective-permute-start | bytes 9437192 | tf_op jit(solution)/shard_map/ppermute | solution.py:252
  82.9 0.4 collective-permute-start.34
  84.5 2.2 %broadcast_select_fusion.1 = bf16[2,768,1024]{2,1,0:T(8,128)(2,1)S(1)} fusion(bf16[2,768,1024]{2,1,0:T(8,128)(2,1)} %collective-permute-done.30, bf16[2,768,1024]{2,1,0:T(8,128)(2,1)} %get-tuple-element.388.own_in, pred[]{:T(512)} %bitcast.3), kind=kLoop, calls=%fused_computation.1 | loop fusion | flops 1572864 | bytes 9437185 | tf_op jit(solution)/shard_map/jit(_where)/select_n | solution.py:294
  86.7 0.0 collective-permute-done.32
  86.7 68.6 %conditional.3 = (bf16[2,768,1024]{2,1,0:T(8,128)(2,1)}, f32[768,1024]{1,0:T(8,128)S(1)}, f32[768,128]{1,0:T(8,128)S(1)}, f32[768,128]{1,0:T(8,128)S(1)}) conditional(s32[]{:T(128)} %bitcast.2, (s32[1]{0:T(128)}, bf16[2,768,1024]{2,1,0:T(8,128)(2,1)S(1)}, bf16[2,768,1024]{2,1,0:T(8,128)(2,1)}, f32[1]{0:T(128)}, ...), branch_computations={%region_15.16_spmd, %region_16.17_spmd, %region_17.18_spmd, %regio... | conditional | flops 7249330176 | bytes 28311624 | solution.py:301
  86.8 1.3 collective-permute-start.15
  88.1 32.5 %branch_1_fun.1 = (f32[768,1024]{1,0:T(8,128)S(1)}, f32[768,128]{1,0:T(8,128)S(1)}, f32[768,128]{1,0:T(8,128)S(1)}) custom-call(f32[1]{0:T(128)} %get-tuple-element.238.h_ref, s32[1]{0:T(128)} %get-tuple-element.239.skip_ref, bf16[2,768,1024]{2,1,0:T(8,128)(2,1)} %get-tuple-element.240.own_in.refs_0_, ...), custom_call_target="tpu_custom_call" | custom-call | flops 7247757312 | bytes 15728640 | tf_op jit(solution)/shard_map/cond/branch_1_fun/pallas_call | solution.py:201
  120.6 34.8 %collective-permute-done.15 = bf16[2,768,1024]{2,1,0:T(8,128)(2,1)} collective-permute-done((bf16[2,768,1024]{2,1,0:T(8,128)(2,1)S(1)}, bf16[2,768,1024]{2,1,0:T(8,128)(2,1)}, u32[]{:S(2)}, u32[]{:S(2)}) %collective-permute-start.15) | collective-permute-done | bytes 3145760 | tf_op jit(solution)/shard_map/cond/branch_1_fun/ppermute | solution.py:252
  155.4 0.0 collective-permute-done.31.refs_2_
  155.4 2.1 %collective-permute-start.33 = (bf16[2,768,1024]{2,1,0:T(8,128)(2,1)S(1)}, bf16[2,768,1024]{2,1,0:T(8,128)(2,1)S(1)}, u32[]{:S(2)}, u32[]{:S(2)}) collective-permute-start(bf16[2,768,1024]{2,1,0:T(8,128)(2,1)S(1)} %collective-permute-done.31.refs_2_), channel_id=1, source_target_pairs={{0,1},{1,0},{2,3},{3,2},{4,5},{5,4},{6,7},{7,6},{8,9},{9,8},{10,11... | collective-permute-start | bytes 9437192 | tf_op jit(solution)/shard_map/ppermute | solution.py:252
  158.1 0.0 collective-permute-done.34.refs_0_
  158.2 11.5 %shard_map.47 = (f32[768,1024]{1,0:T(8,128)S(1)}, f32[768,128]{1,0:T(8,128)S(1)}) custom-call(f32[1]{0:T(128)S(6)} %copy.84.h_ref, s32[1]{0:T(128)} %get-tuple-element.387.flag_ref, bf16[2,768,1024]{2,1,0:T(8,128)(2,1)} %get-tuple-element.388.own_in, bf16[2,768,1024]{2,1,0:T(8,128)(2,1)} %collective-permute-done.34.refs_0_, ...), custom_call_target="tpu_custom_call" | custom-call | flops 7247757312 | bytes 15728640 | tf_op jit(solution)/shard_map/pallas_call | solution.py:228
  169.7 0.0 collective-permute-done.33.refs_0_
  169.7 8.1 %shard_map.48 = f32[768,1024]{1,0:T(8,128)} custom-call(f32[1]{0:T(128)S(6)} %copy.84.h_ref, s32[1]{0:T(128)} %get-tuple-element.387.flag_ref, bf16[2,768,1024]{2,1,0:T(8,128)(2,1)} %get-tuple-element.388.own_in, bf16[2,768,1024]{2,1,0:T(8,128)(2,1)S(1)} %collective-permute-done.33.refs_0_, f32[768,128]{1,0:T(8,128)S(1)} %get-tuple-element.396.refs_3_.refs_1_, ...), custom_call_target="tpu_custom_call" | custom-call | flops 2415919104 | bytes 9437184 | tf_op jit(solution)/shard_map/pallas_call | solution.py:228
Async XLA Ops:
  4.2 76.8 %collective-permute-start.30 = (bf16[2,768,1024]{2,1,0:T(8,128)(2,1)}, bf16[2,768,1024]{2,1,0:T(8,128)(2,1)}, u32[]{:S(2)}, u32[]{:S(2)}) collective-permute-start(bf16[2,768,1024]{2,1,0:T(8,128)(2,1)} %get-tuple-element.388.own_in), channel_id=1, source_target_pairs={{0,64},{1,65},{2,66},{3,67},{4,68},{5,69},{6,70},{7,71},{8,72},{9,... | collective-permute-start | bytes 9437192 | tf_op jit(solution)/shard_map/ppermute | solution.py:252
  6.4 80.3 %collective-permute-start.32 = (bf16[2,768,1024]{2,1,0:T(8,128)(2,1)}, bf16[2,768,1024]{2,1,0:T(8,128)(2,1)}, u32[]{:S(2)}, u32[]{:S(2)}) collective-permute-start(bf16[2,768,1024]{2,1,0:T(8,128)(2,1)} %get-tuple-element.388.own_in), channel_id=1, source_target_pairs={{0,1},{1,0},{2,3},{3,2},{4,5},{5,4},{6,7},{7,6},{8,9},{9,8},{10,11... | collective-permute-start | bytes 9437192 | tf_op jit(solution)/shard_map/ppermute | solution.py:252
  8.1 72.9 %collective-permute-start.8 = (bf16[2,768,1024]{2,1,0:T(8,128)(2,1)}, bf16[2,768,1024]{2,1,0:T(8,128)(2,1)}, u32[]{:S(2)}, u32[]{:S(2)}) collective-permute-start(bf16[2,768,1024]{2,1,0:T(8,128)(2,1)} %param.8), channel_id=1, source_target_pairs={{0,36},{1,37},{2,38},{3,39},{4,32},{5,33},{6,34},{7,35},{8,44},{9,... | collective-permute-start | bytes 9437192 | tf_op jit(solution)/shard_map/cond/branch_8_fun/ppermute | solution.py:252
  81.0 74.4 %collective-permute-start.31 = (bf16[2,768,1024]{2,1,0:T(8,128)(2,1)}, bf16[2,768,1024]{2,1,0:T(8,128)(2,1)S(1)}, u32[]{:S(2)}, u32[]{:S(2)}) collective-permute-start(bf16[2,768,1024]{2,1,0:T(8,128)(2,1)} %collective-permute-done.30), channel_id=1, source_target_pairs={{0,66},{1,67},{2,64},{3,65},{4,70},{5,71},{6,68},{7,69},{8,74},{9,... | collective-permute-start | bytes 9437192 | tf_op jit(solution)/shard_map/ppermute | solution.py:252
  82.9 75.2 %collective-permute-start.34 = (bf16[2,768,1024]{2,1,0:T(8,128)(2,1)}, bf16[2,768,1024]{2,1,0:T(8,128)(2,1)}, u32[]{:S(2)}, u32[]{:S(2)}) collective-permute-start(bf16[2,768,1024]{2,1,0:T(8,128)(2,1)} %get-tuple-element.466), channel_id=1, source_target_pairs={{0,64},{1,65},{2,66},{3,67},{4,68},{5,69},{6,70},{7,71},{8,72},{9,... | collective-permute-start | bytes 9437192 | tf_op jit(solution)/shard_map/ppermute | solution.py:252
  86.8 68.6 %collective-permute-start.15 = (bf16[2,768,1024]{2,1,0:T(8,128)(2,1)S(1)}, bf16[2,768,1024]{2,1,0:T(8,128)(2,1)}, u32[]{:S(2)}, u32[]{:S(2)}) collective-permute-start(bf16[2,768,1024]{2,1,0:T(8,128)(2,1)S(1)} %get-tuple-element.237), channel_id=1, source_target_pairs={{0,4},{1,5},{2,6},{3,7},{4,0},{5,1},{6,2},{7,3},{8,12},{9,13},{10,... | collective-permute-start | bytes 9437192 | tf_op jit(solution)/shard_map/cond/branch_1_fun/ppermute | solution.py:252
  155.4 14.3 %collective-permute-start.33 = (bf16[2,768,1024]{2,1,0:T(8,128)(2,1)S(1)}, bf16[2,768,1024]{2,1,0:T(8,128)(2,1)S(1)}, u32[]{:S(2)}, u32[]{:S(2)}) collective-permute-start(bf16[2,768,1024]{2,1,0:T(8,128)(2,1)S(1)} %collective-permute-done.31.refs_2_), channel_id=1, source_target_pairs={{0,1},{1,0},{2,3},{3,2},{4,5},{5,4},{6,7},{7,6},{8,9},{9,8},{10,11... | collective-permute-start | bytes 9437192 | tf_op jit(solution)/shard_map/ppermute | solution.py:252
